TPU v7x, 128 devices: a whole 4x4x4 slice. The times are simulated.
128 devices in a mesh: gx: 16 (over y, x), gy: 8 (over z, core).
Axes of the slice: x: 4, y: 4, z: 4, core: 2. Of those that a mesh axis runs over, the one named last changes fastest.
Arguments:
- initial_state: float32 [16384, 16384], P(('gx', 'gy')), may hold values from -16 to 16
- edge_list: int32 [56, 2], replicated, may hold values from 0 to 27, as said below
- couplings: float32 [56], replicated, may hold values from -0.15 to 0.15
- gates_low: float32 [6, 128, 128], replicated, may hold values from -2 to 2
- gates_mid: float32 [6, 128, 128], replicated, may hold values from -2 to 2
- gates_high: float32 [6, 128, 128], replicated, may hold values from -2 to 2
- top_gate: float32 [128, 128], replicated, may hold values from -2 to 2
Outputs:
- evolved: float32 [16384, 16384], P(('gx', 'gy'))
Inputs may be any that keep to these rules, and one draw needn't show every extreme that they name: `edge_list`: each row names two different spins; every spin is named by some row.
All inputs are finite; a program needn't handle non-finite values.
Results may differ from a plain program's by a relative error of at most 0.0003.
Values sent between devices are 32-bit elements; how exact they have to be, the bound alone decides.
No kernel may reach another device: no remote copies, remote signals or barrier semaphores. Data moves between devices by JAX's collectives and lax.ppermute only.
A program may use at most 128 MiB of HBM per device.

v0:
```python
import jax
import jax.numpy as jnp
from jax import lax
from jax.sharding import PartitionSpec as P

highest = lax.Precision.HIGHEST


def spin_signs(index_list, bit_count):
    shift_amounts = bit_count - 1 - jnp.arange(bit_count, dtype=jnp.int32)
    bit_values = jnp.right_shift(index_list[:, None], shift_amounts[None, :]) & 1
    return (1 - 2 * bit_values).astype(jnp.float32)


def coupling_matrix(edge_list, couplings, qubit_count):
    qubit_names = jnp.arange(qubit_count, dtype=jnp.int32)
    first_end = (edge_list[:, 0:1] == qubit_names[None, :]).astype(jnp.float32)
    second_end = (edge_list[:, 1:2] == qubit_names[None, :]).astype(jnp.float32)
    return jnp.dot((first_end * couplings[:, None]).T, second_end, precision=highest)


def energy_field(row_ids, row_bits, col_ids, col_bits, matrix):
    row_spins = spin_signs(row_ids, row_bits)
    col_spins = spin_signs(col_ids, col_bits)
    row_block = matrix[:row_bits, :row_bits]
    col_block = matrix[row_bits:, row_bits:]
    mixed_block = matrix[:row_bits, row_bits:] + matrix[row_bits:, :row_bits].T
    row_energy = jnp.sum(jnp.dot(row_spins, row_block, precision=highest) * row_spins, axis=1)
    col_energy = jnp.sum(jnp.dot(col_spins, col_block, precision=highest) * col_spins, axis=1)
    cross_term = jnp.dot(
        jnp.dot(row_spins, mixed_block, precision=highest), col_spins.T, precision=highest
    )
    return row_energy[:, None] + col_energy[None, :] + cross_term


def local(initial_state, edge_list, couplings, gates_low, gates_mid, gates_high, top_gate):
    size_x = lax.axis_size("gx")
    size_y = lax.axis_size("gy")
    devices = size_x * size_y
    global_bits = devices.bit_length() - 1
    high_rows = initial_state.shape[0]
    plane_size = initial_state.shape[1]
    block_width = gates_low.shape[1]
    high_bits = high_rows.bit_length() - 1
    block_bits = block_width.bit_length() - 1
    row_bits = global_bits + high_bits
    col_bits = 2 * block_bits
    sliver = high_rows // devices
    matrix = coupling_matrix(edge_list, couplings, row_bits + col_bits)
    position = lax.axis_index("gx") * size_y + lax.axis_index("gy")
    col_ids = jnp.arange(plane_size, dtype=jnp.int32)
    local_rows = position * high_rows + jnp.arange(high_rows, dtype=jnp.int32)
    factor = jnp.exp(energy_field(local_rows, row_bits, col_ids, col_bits, matrix))
    amplitudes = initial_state
    for layer_index in range(gates_low.shape[0]):
        amplitudes = amplitudes * factor
        amplitudes = jnp.dot(
            amplitudes.reshape(high_rows * block_width, block_width),
            gates_low[layer_index].T,
            precision=highest,
        )
        amplitudes = jnp.matmul(
            gates_mid[layer_index][None],
            amplitudes.reshape(high_rows, block_width, block_width),
            precision=highest,
        )
        amplitudes = jnp.dot(
            gates_high[layer_index], amplitudes.reshape(high_rows, plane_size), precision=highest
        )
    exchanged = lax.all_to_all(
        amplitudes.reshape(1, high_rows, plane_size),
        ("gx", "gy"),
        split_axis=1,
        concat_axis=0,
        tiled=True,
    )
    exchanged = exchanged.reshape(high_rows, plane_size)
    rotated = jnp.dot(top_gate, exchanged, precision=highest)
    restored = lax.all_to_all(
        rotated.reshape(devices, sliver, plane_size),
        ("gx", "gy"),
        split_axis=0,
        concat_axis=1,
        tiled=True,
    )
    restored = restored.reshape(high_rows, plane_size)
    restored = restored * factor
    squares_total = lax.psum(jnp.sum(restored * restored), ("gx", "gy"))
    mean_square = squares_total / jnp.float32(devices * high_rows * plane_size)
    return restored / jnp.sqrt(mean_square + 1e-06)


def solution(mesh):
    in_specs = (P(("gx", "gy"), None), P(), P(), P(), P(), P(), P())
    out_specs = P(("gx", "gy"), None)
    return jax.shard_map(local, mesh=mesh, in_specs=in_specs, out_specs=out_specs, check_vma=False)
```

profile of v0, /device:TPU:1, one launch (start us, length us, event | category | flops | bytes accessed | tf_op | source)
XLA Modules:
  0.0 637.0 jit_solution(10312082110424259234)
XLA Ops:
  0.0 0.8 slice_bitcast_fusion.2
  0.8 0.9 fusion.65
  1.7 0.1 slice.98
  1.8 1.5 fusion.13
  3.3 0.2 fusion.14
  3.5 0.1 copy.61
  3.6 0.2 fusion.72
  3.8 9.8 %fusion.5 = f32[128,16384]{1,0:T(8,128)} fusion(f32[128,14]{0,1:T(8,128)S(1)} %fusion.72, f32[16384]{0:T(1024)S(1)} %fusion.13, f32[128]{0:T(128)S(1)} %fusion.14, s32[14]{0:T(128)S(1)} %iota_subtract_fusion), kind=kOutput, calls=%fused_computation.13 | convolution fusion | flops 357662720 | bytes 8461880 | tf_op jit(solution)/shard_map/dot_general | solution.py:30
  13.7 10.0 %multiply_bitcast_fusion = f32[16,8,128,128]{3,1,2,0:T(8,128)} fusion(f32[128,16384]{1,0:T(8,128)} %param.7, f32[128,16384]{1,0:T(8,128)} %fusion.5), kind=kLoop, calls=%fused_computation.19 | loop fusion | flops 2097152 | bytes 25165824
  23.7 4.9 copy.62
  28.6 8.3 %fusion.45 = f32[128,128,128]{1,2,0:T(8,128)S(1)} fusion(f32[128,128,128]{2,1,0:T(8,128)S(1)} %bitcast.184, f32[6,128,128]{2,1,0:T(8,128)S(1)} %copy-done.2), kind=kOutput, calls=%fused_computation.66 | convolution fusion | flops 3221225472 | bytes 16842752 | tf_op jit(solution)/shard_map/dot_general | solution.py:57
  37.0 9.1 %convolution_bitcast_fusion.12 = f32[128,128,128]{1,2,0:T(8,128)} fusion(f32[128,128,128]{1,2,0:T(8,128)S(1)} %fusion.45, f32[6,128,128]{2,1,0:T(8,128)S(1)} %copy-done.3), kind=kOutput, calls=%fused_computation.31 | convolution fusion | flops 3221225472 | bytes 16842752 | tf_op jit(solution)/shard_map/dot_general | solution.py:62
  46.1 9.4 %copy.30 = f32[128,128,128]{0,2,1:T(8,128)} copy(f32[128,128,128]{1,2,0:T(8,128)} %convolution_bitcast_fusion.12) | data formatting | bytes 16777216 | tf_op jit(solution)/shard_map/transpose | solution.py:62
  55.5 12.6 %fusion.8 = f32[16,8,128,128]{3,1,2,0:T(8,128)S(1)} fusion(f32[128,16384]{1,0:T(8,128)} %fusion.5, f32[128,16384]{0,1:T(8,128)} %bitcast.178, f32[6,128,128]{2,1,0:T(8,128)S(1)} %copy-done.4), kind=kOutput, calls=%fused_computation.21 | convolution fusion | flops 3223322624 | bytes 25231360 | tf_op jit(solution)/shard_map/dot_general | solution.py:67
  68.1 1.5 copy.63
  69.6 8.3 %fusion.41 = f32[128,128,128]{1,2,0:T(8,128)S(1)} fusion(f32[128,128,128]{2,1,0:T(8,128)S(1)} %bitcast.185, f32[6,128,128]{2,1,0:T(8,128)S(1)} %copy-done.2), kind=kOutput, calls=%fused_computation.62 | convolution fusion | flops 3221225472 | bytes 16842752 | tf_op jit(solution)/shard_map/dot_general | solution.py:57
  77.9 9.0 %convolution_bitcast_fusion.11 = f32[128,128,128]{1,2,0:T(8,128)} fusion(f32[128,128,128]{1,2,0:T(8,128)S(1)} %fusion.41, f32[6,128,128]{2,1,0:T(8,128)S(1)} %copy-done.3), kind=kOutput, calls=%fused_computation.30 | convolution fusion | flops 3221225472 | bytes 16842752 | tf_op jit(solution)/shard_map/dot_general | solution.py:62
  86.9 9.3 %copy.33 = f32[128,128,128]{0,2,1:T(8,128)} copy(f32[128,128,128]{1,2,0:T(8,128)} %convolution_bitcast_fusion.11) | data formatting | bytes 16777216 | tf_op jit(solution)/shard_map/transpose | solution.py:62
  96.3 12.4 %fusion.9 = f32[16,8,128,128]{3,1,2,0:T(8,128)S(1)} fusion(f32[128,16384]{1,0:T(8,128)} %fusion.5, f32[128,16384]{0,1:T(8,128)} %bitcast.179, f32[6,128,128]{2,1,0:T(8,128)S(1)} %copy-done.4), kind=kOutput, calls=%fused_computation.22 | convolution fusion | flops 3223322624 | bytes 25231360 | tf_op jit(solution)/shard_map/dot_general | solution.py:67
  108.6 1.5 copy.64
  110.1 8.3 %fusion.37 = f32[128,128,128]{1,2,0:T(8,128)S(1)} fusion(f32[128,128,128]{2,1,0:T(8,128)S(1)} %bitcast.186, f32[6,128,128]{2,1,0:T(8,128)S(1)} %copy-done.2), kind=kOutput, calls=%fused_computation.58 | convolution fusion | flops 3221225472 | bytes 16842752 | tf_op jit(solution)/shard_map/dot_general | solution.py:57
  118.5 9.1 %convolution_bitcast_fusion.10 = f32[128,128,128]{1,2,0:T(8,128)} fusion(f32[128,128,128]{1,2,0:T(8,128)S(1)} %fusion.37, f32[6,128,128]{2,1,0:T(8,128)S(1)} %copy-done.3), kind=kOutput, calls=%fused_computation.29 | convolution fusion | flops 3221225472 | bytes 16842752 | tf_op jit(solution)/shard_map/dot_general | solution.py:62
  127.6 9.3 %copy.36 = f32[128,128,128]{0,2,1:T(8,128)} copy(f32[128,128,128]{1,2,0:T(8,128)} %convolution_bitcast_fusion.10) | data formatting | bytes 16777216 | tf_op jit(solution)/shard_map/transpose | solution.py:62
  136.9 12.6 %fusion.10 = f32[16,8,128,128]{3,1,2,0:T(8,128)S(1)} fusion(f32[128,16384]{1,0:T(8,128)} %fusion.5, f32[128,16384]{0,1:T(8,128)} %bitcast.180, f32[6,128,128]{2,1,0:T(8,128)S(1)} %copy-done.4), kind=kOutput, calls=%fused_computation.23 | convolution fusion | flops 3223322624 | bytes 25231360 | tf_op jit(solution)/shard_map/dot_general | solution.py:67
  149.5 1.5 copy.65
  151.0 8.3 %fusion.33 = f32[128,128,128]{1,2,0:T(8,128)S(1)} fusion(f32[128,128,128]{2,1,0:T(8,128)S(1)} %bitcast.187, f32[6,128,128]{2,1,0:T(8,128)S(1)} %copy-done.2), kind=kOutput, calls=%fused_computation.54 | convolution fusion | flops 3221225472 | bytes 16842752 | tf_op jit(solution)/shard_map/dot_general | solution.py:57
  159.3 9.0 %convolution_bitcast_fusion.9 = f32[128,128,128]{1,2,0:T(8,128)} fusion(f32[128,128,128]{1,2,0:T(8,128)S(1)} %fusion.33, f32[6,128,128]{2,1,0:T(8,128)S(1)} %copy-done.3), kind=kOutput, calls=%fused_computation.28 | convolution fusion | flops 3221225472 | bytes 16842752 | tf_op jit(solution)/shard_map/dot_general | solution.py:62
  168.3 9.3 %copy.39 = f32[128,128,128]{0,2,1:T(8,128)} copy(f32[128,128,128]{1,2,0:T(8,128)} %convolution_bitcast_fusion.9) | data formatting | bytes 16777216 | tf_op jit(solution)/shard_map/transpose | solution.py:62
  177.7 12.4 %fusion.11 = f32[16,8,128,128]{3,1,2,0:T(8,128)S(1)} fusion(f32[128,16384]{1,0:T(8,128)} %fusion.5, f32[128,16384]{0,1:T(8,128)} %bitcast.181, f32[6,128,128]{2,1,0:T(8,128)S(1)} %copy-done.4), kind=kOutput, calls=%fused_computation.24 | convolution fusion | flops 3223322624 | bytes 25231360 | tf_op jit(solution)/shard_map/dot_general | solution.py:67
  190.0 1.5 copy.66
  191.5 8.3 %fusion.29 = f32[128,128,128]{1,2,0:T(8,128)S(1)} fusion(f32[128,128,128]{2,1,0:T(8,128)S(1)} %bitcast.188, f32[6,128,128]{2,1,0:T(8,128)S(1)} %copy-done.2), kind=kOutput, calls=%fused_computation.50 | convolution fusion | flops 3221225472 | bytes 16842752 | tf_op jit(solution)/shard_map/dot_general | solution.py:57
  199.9 9.1 %convolution_bitcast_fusion.8 = f32[128,128,128]{1,2,0:T(8,128)} fusion(f32[128,128,128]{1,2,0:T(8,128)S(1)} %fusion.29, f32[6,128,128]{2,1,0:T(8,128)S(1)} %copy-done.3), kind=kOutput, calls=%fused_computation.27 | convolution fusion | flops 3221225472 | bytes 16842752 | tf_op jit(solution)/shard_map/dot_general | solution.py:62
  209.0 9.3 %copy.42 = f32[128,128,128]{0,2,1:T(8,128)} copy(f32[128,128,128]{1,2,0:T(8,128)} %convolution_bitcast_fusion.8) | data formatting | bytes 16777216 | tf_op jit(solution)/shard_map/transpose | solution.py:62
  218.3 12.6 %fusion.12 = f32[16,8,128,128]{3,1,2,0:T(8,128)S(1)} fusion(f32[128,16384]{1,0:T(8,128)} %fusion.5, f32[128,16384]{0,1:T(8,128)} %bitcast.182, f32[6,128,128]{2,1,0:T(8,128)S(1)} %copy-done.4), kind=kOutput, calls=%fused_computation.25 | convolution fusion | flops 3223322624 | bytes 25231360 | tf_op jit(solution)/shard_map/dot_general | solution.py:67
  230.9 1.5 copy.67
  232.4 8.3 %fusion.25 = f32[128,128,128]{1,2,0:T(8,128)S(1)} fusion(f32[128,128,128]{2,1,0:T(8,128)S(1)} %bitcast.189, f32[6,128,128]{2,1,0:T(8,128)S(1)} %copy-done.2), kind=kOutput, calls=%fused_computation.46 | convolution fusion | flops 3221225472 | bytes 16842752 | tf_op jit(solution)/shard_map/dot_general | solution.py:57
  240.7 9.0 %convolution_bitcast_fusion.7 = f32[128,128,128]{1,2,0:T(8,128)} fusion(f32[128,128,128]{1,2,0:T(8,128)S(1)} %fusion.25, f32[6,128,128]{2,1,0:T(8,128)S(1)} %copy-done.3), kind=kOutput, calls=%fused_computation.26 | convolution fusion | flops 3221225472 | bytes 16842752 | tf_op jit(solution)/shard_map/dot_general | solution.py:62
  249.7 9.4 %copy.45 = f32[128,128,128]{0,2,1:T(8,128)} copy(f32[128,128,128]{1,2,0:T(8,128)} %convolution_bitcast_fusion.7) | data formatting | bytes 16777216 | tf_op jit(solution)/shard_map/transpose | solution.py:62
  259.1 16.9 %convolution_bitcast_fusion.1 = f32[1,128,16384]{1,2,0:T(8,128)} fusion(f32[128,16384]{0,1:T(8,128)} %bitcast.183, f32[6,128,128]{2,1,0:T(8,128)S(1)} %copy-done.4), kind=kOutput, calls=%fused_computation.1 | convolution fusion | flops 3221225472 | bytes 16842752 | tf_op jit(solution)/shard_map/dot_general | solution.py:67
  276.0 18.1 %copy.46 = f32[1,128,16384]{2,0,1:T(1,128)} copy(f32[1,128,16384]{1,2,0:T(8,128)} %convolution_bitcast_fusion.1) | data formatting | bytes 16777216 | tf_op jit(solution)/shard_map/reshape | solution.py:71
  294.0 110.4 %all_to_all.8 = f32[1,128,16384]{2,0,1:T(1,128)S(1)} all-to-all(f32[1,128,16384]{2,0,1:T(1,128)} %copy.46), channel_id=1, replica_groups=mesh['gx'=16,'gy'=8] {'gx','gy'}, dimensions={1} | all-to-all | bytes 16777216 | tf_op jit(solution)/shard_map/all_to_all | solution.py:70
  404.4 17.9 %convolution_bitcast_fusion = f32[128,1,16384]{0,2,1:T(8,128)} fusion(f32[128,128]{1,0:T(8,128)S(1)} %copy-done, f32[1,128,16384]{2,0,1:T(1,128)S(1)} %all_to_all.8), kind=kOutput, calls=%fused_computation | convolution fusion | flops 3221225472 | bytes 16842752 | tf_op jit(solution)/shard_map/dot_general | solution.py:78
  422.3 18.0 %copy.47 = f32[128,1,16384]{2,1,0:T(1,128)} copy(f32[128,1,16384]{0,2,1:T(8,128)} %convolution_bitcast_fusion) | data formatting | bytes 16777216 | tf_op jit(solution)/shard_map/reshape | solution.py:80
  440.3 104.3 %all_to_all.9 = f32[128,1,16384]{2,1,0:T(1,128)S(1)} all-to-all(f32[128,1,16384]{2,1,0:T(1,128)} %copy.47), channel_id=1, replica_groups=mesh['gx'=16,'gy'=8] {'gx','gy'}, dimensions={0} | all-to-all | bytes 16777216 | tf_op jit(solution)/shard_map/all_to_all | solution.py:79
  544.7 3.2 copy-done.1
  547.9 11.0 %multiply_reduce_fusion = f32[]{:T(128)} fusion(f32[128,16384]{1,0:T(8,128)} %fusion.5, f32[128,1,16384]{2,1,0:T(1,128)S(1)} %all_to_all.9), kind=kLoop, calls=%fused_computation.18 | loop fusion | flops 6291455 | bytes 16777220 | tf_op jit(solution)/shard_map/reduce_sum | solution.py:88
  558.9 63.9 %psum.7 = f32[]{:T(128)} all-reduce(f32[]{:T(128)} %multiply_reduce_fusion), channel_id=1, replica_groups=mesh['gx'=16,'gy'=8] {'gx','gy'}, use_global_device_ids=true, to_apply=%region_3.0 | all-reduce | flops 1 | bytes 8 | tf_op jit(solution)/shard_map/psum | solution.py:88
  623.4 13.1 %broadcast_divide_fusion = f32[128,16384]{1,0:T(8,128)} fusion(f32[]{:T(128)S(6)} %sqrt.3, f32[128,16384]{1,0:T(8,128)} %fusion.5, f32[128,1,16384]{2,1,0:T(1,128)} %copy-done.1), kind=kLoop, calls=%fused_computation.20 | loop fusion | flops 4194304 | bytes 25165828 | tf_op jit(solution)/shard_map/div | solution.py:90
  (11 shorter events, 0.0 us)
Async XLA Ops:
  0.0 404.4 %copy-start = (f32[128,128]{1,0:T(8,128)S(1)}, f32[128,128]{1,0:T(8,128)}, u32[]{:S(2)}) copy-start(f32[128,128]{1,0:T(8,128)} %param.13) | copy-start | bytes 196612
  23.7 4.9 copy-start.2
  28.6 8.4 %copy-start.3 = (f32[6,128,128]{2,1,0:T(8,128)S(1)}, f32[6,128,128]{2,1,0:T(8,128)}, u32[]{:S(2)}) copy-start(f32[6,128,128]{2,1,0:T(8,128)} %param.11) | copy-start | bytes 1179652
  46.1 9.4 %copy-start.4 = (f32[6,128,128]{2,1,0:T(8,128)S(1)}, f32[6,128,128]{2,1,0:T(8,128)}, u32[]{:S(2)}) copy-start(f32[6,128,128]{2,1,0:T(8,128)} %param.12) | copy-start | bytes 1179652
  544.7 3.2 copy-start.1
where the time goes:
time: 643 us; the launch traced here: 637 us
  blocking collectives  279 us (43%)
  matrix products  214 us (33%)
  local copies, waits for them, and re-layouts  108 us (17%)
  other arithmetic  34.1 us (5%)
    all_to_all x1, blocking collectives, local(): lax.all_to_all(amplitudes.reshape(1, high_rows, plane_size), ('gx', 'gy')...  110 us
    all_to_all x1, blocking collectives, local(): lax.all_to_all(rotated.reshape(devices, sliver, plane_size), ('gx', 'gy')...  104 us
    dot_general x6, matrix products, local(): jnp.dot(gates_high[layer_index], amplitudes.reshape(high_rows, plane_size...  79.5 us
    psum x1, blocking collectives, local(): squares_total = lax.psum(jnp.sum(restored * restored), ('gx', 'gy'))  63.9 us
    transpose x6, local copies, waits for them, and re-layouts, local(): jnp.matmul(gates_mid[layer_index][None], amplitudes.reshape(high_rows, bl...  56 us
    dot_general x6, matrix products, local(): jnp.matmul(gates_mid[layer_index][None], amplitudes.reshape(high_rows, bl...  54.3 us
    dot_general x6, matrix products, local(): jnp.dot(amplitudes.reshape(high_rows * block_width, block_width), gates_l...  50.1 us
    reshape x1, local copies, waits for them, and re-layouts, local(): amplitudes.reshape(1, high_rows, plane_size)  18.1 us

commit v1 on v0

v1 whole, which is shorter than its diff:
```python
import jax
import jax.numpy as jnp
from jax import lax
from jax.experimental import pallas as pl
from jax.experimental.pallas import tpu as pltpu
from jax.sharding import PartitionSpec as P

HIGHEST = lax.Precision.HIGHEST
F32 = jnp.float32
BF16 = jnp.bfloat16
N = 128
BITS = 7
LAYERS = 6
AXES = ("gx", "gy")
GROUP = 32
PITCH = N + 8
MIX_GROUP = 16
PIECE = 8
VMEM_BYTES = 62 * 2**20


def mm(a, b):
    return lax.dot_general(a, b, (((1,), (0,)), ((), ())), preferred_element_type=F32)


def mm_exact(a, b):
    return jnp.dot(a, b, precision=HIGHEST, preferred_element_type=F32)


def mm_nt_exact(a, b):
    return lax.dot_general(
        a, b, (((1,), (1,)), ((), ())), precision=HIGHEST, preferred_element_type=F32
    )


def iota(axis):
    return lax.broadcasted_iota(jnp.int32, (N, N), axis)


def split(x):
    high = x.astype(BF16)
    low = (x - high.astype(F32)).astype(BF16)
    return high, low


def left_pack(gate):
    high, low = split(gate)
    return jnp.concatenate(
        [jnp.concatenate([high, high], axis=1), jnp.concatenate([low, low], axis=1)], axis=0
    )


def right_pack(gate):
    high, low = split(gate.T)
    row = jnp.concatenate([high, low], axis=1)
    return jnp.concatenate([row, row], axis=0)


def left_gate(pack, tiles):
    out = []
    for i in range(0, len(tiles), 2):
        high, low = split(jnp.concatenate(tiles[i : i + 2], axis=1))
        both = mm(pack, jnp.concatenate([high, low], axis=0))
        both = both[:N] + both[N:]
        out += [both[:, :N], both[:, N:]]
    return out


def right_gate(pack, tiles):
    out = []
    for i in range(0, len(tiles), 2):
        high, low = split(jnp.concatenate(tiles[i : i + 2], axis=0))
        both = mm(jnp.concatenate([high, low], axis=1), pack)
        both = both[:, :N] + both[:, N:]
        out += [both[:N], both[N:]]
    return out


def spins(start, value):
    qubit = iota(1)
    inside = (qubit >= start) & (qubit < start + BITS)
    shift = jnp.clip(start + BITS - 1 - qubit, 0, BITS - 1)
    bit = jnp.right_shift(value, shift) & 1
    return jnp.where(inside, 1 - 2 * bit, 0).astype(F32)


def coupling_matrix(edge_ref, coupling_ref):
    names = lax.broadcasted_iota(jnp.int32, (N, edge_ref.shape[1]), 0)
    first = (edge_ref[0:1, :] == names).astype(F32) * coupling_ref[...]
    second = (edge_ref[1:2, :] == names).astype(F32)
    one_way = mm_nt_exact(first, second)
    return one_way + one_way.T


def flat_position():
    return lax.axis_index("gx") * lax.axis_size("gy") + lax.axis_index("gy")


def pair_factors(matrix, fixed, rows, planes, lanes):
    row_field = mm_exact(rows, matrix)
    plane_field = mm_exact(planes, matrix)
    row_fixed = rows + fixed
    row_energy = jnp.sum(0.5 * mm_exact(row_fixed, matrix) * row_fixed, axis=1, keepdims=True)
    plane_energy = jnp.sum(plane_field * (0.5 * planes + fixed), axis=1, keepdims=True)
    lane_terms = mm_exact(lanes, matrix) * (0.5 * lanes + fixed)
    lane_energy = mm_nt_exact(jnp.ones((N, N), F32), lane_terms)
    over_lanes = jnp.exp(mm_nt_exact(row_field, lanes) + row_energy)
    over_rows = jnp.exp(mm_nt_exact(row_field, planes))
    over_planes = jnp.exp(mm_nt_exact(plane_field, lanes) + plane_energy + lane_energy)
    return over_lanes, over_rows, over_planes


def plane_tile(plane):
    return pl.ds(pl.multiple_of(plane * PITCH, 8), N)


def row_tile(row):
    return pl.ds(row, N, stride=PITCH)


def each(count, body):
    def step(i, c):
        body(i)
        return c

    lax.fori_loop(0, count, step, 0)


def sweep(body):
    each(N // GROUP, lambda i: body(i * GROUP))


def start_copies(sem, *pairs):
    copies = [pltpu.make_async_copy(source, target, sem.at[i]) for i, (source, target) in enumerate(pairs)]
    for copy in copies:
        copy.start()
    return copies


def evolve_kernel(edge_hbm, coupling_hbm, low_hbm, mid_hbm, high_hbm, state_ref, out_ref,
                  by_plane, by_row, factor, edge_ref, coupling_ref, low_ref, mid_ref, high_ref,
                  lane_part, plane_part, turning, packs, small_sem, in_sem, out_sem):
    def load(plane):
        columns = pl.ds(pl.multiple_of(plane * N, N), N)
        return pltpu.make_async_copy(state_ref.at[:, columns], by_plane.at[plane_tile(plane)], in_sem.at[plane])

    def store(plane):
        return pltpu.make_async_copy(by_plane.at[plane_tile(plane)], out_ref.at[plane], out_sem.at[plane])

    small = start_copies(
        small_sem,
        (edge_hbm, edge_ref), (coupling_hbm, coupling_ref),
        (high_hbm, high_ref), (low_hbm, low_ref), (mid_hbm, mid_ref),
    )
    each(N, lambda plane: load(plane).start())
    for copy in small[:2]:
        copy.wait()
    matrix = coupling_matrix(edge_ref, coupling_ref)
    lane_part[...], turning[...], plane_part[...] = pair_factors(
        matrix,
        spins(0, flat_position()),
        spins(BITS, iota(0)),
        spins(2 * BITS, iota(0)),
        spins(3 * BITS, iota(0)),
    )
    for copy in small[2:]:
        copy.wait()
    packs[0] = left_pack(high_ref[0])
    packs[1] = right_pack(low_ref[0])

    def first(plane):
        each(GROUP, lambda j: load(plane + j).wait())
        columns = turning[...]
        tiles = []
        for j in range(GROUP):
            scale = lane_part[...] * (plane_part[pl.ds(plane + j, 1), :] * columns[:, j : j + 1])
            factor[plane_tile(plane + j)] = scale
            tiles.append(by_plane[plane_tile(plane + j)] * scale)
        turning[...] = pltpu.roll(columns, N - GROUP, 1)
        tiles = right_gate(packs[1], left_gate(packs[0], tiles))
        for j in range(GROUP):
            by_plane[plane_tile(plane + j)] = tiles[j]

    sweep(first)

    for layer in range(1, LAYERS):
        rows_now = layer % 2 == 1
        across = mid_ref if rows_now else high_ref
        packs[0] = left_pack(across[layer - 1])
        packs[1] = left_pack(across[layer])
        packs[2] = right_pack(low_ref[layer])
        source, target = (by_plane, by_row) if rows_now else (by_row, by_plane)
        factor_tile = row_tile if rows_now else plane_tile

        def middle(index, source=source, target=target, factor_tile=factor_tile):
            tiles = [source[row_tile(index + j)] for j in range(GROUP)]
            tiles = left_gate(packs[0], tiles)
            tiles = [t * factor[factor_tile(index + j)] for j, t in enumerate(tiles)]
            tiles = right_gate(packs[2], left_gate(packs[1], tiles))
            for j in range(GROUP):
                target[plane_tile(index + j)] = tiles[j]

        sweep(middle)

    packs[0] = left_pack(high_ref[LAYERS - 1])

    def last(plane):
        tiles = left_gate(packs[0], [by_row[row_tile(plane + j)] for j in range(GROUP)])
        for j in range(GROUP):
            by_plane[plane_tile(plane + j)] = tiles[j]
        each(GROUP, lambda j: store(plane + j).start())

    sweep(last)
    each(N, lambda plane: store(plane).wait())


def mix_kernel(edge_hbm, coupling_hbm, top_hbm, in_ref, out_ref,
               tiles_in, tiles_out, squares, edge_ref, coupling_ref, top_ref, lane_part, plane_part, turning, pack,
               small_sem, in_sem, out_sem, squares_sem):
    def load(row):
        return pltpu.make_async_copy(in_ref.at[:, row], tiles_in.at[row], in_sem.at[row])

    def store(row):
        return pltpu.make_async_copy(tiles_out.at[row], out_ref.at[:, row], out_sem.at[row])

    small = start_copies(small_sem, (edge_hbm, edge_ref), (coupling_hbm, coupling_ref), (top_hbm, top_ref))
    each(N, lambda row: load(row).start())
    for copy in small:
        copy.wait()
    matrix = coupling_matrix(edge_ref, coupling_ref)
    lane_part[...], turning[...], plane_part[...] = pair_factors(
        matrix,
        spins(2 * BITS, flat_position()),
        spins(0, iota(0)),
        spins(BITS, iota(0)),
        spins(3 * BITS, iota(0)),
    )
    pack[...] = left_pack(top_ref[...])

    def turn(i, total):
        row = i * MIX_GROUP
        each(MIX_GROUP, lambda j: load(row + j).wait())
        columns = turning[...]
        tiles = left_gate(pack[...], [tiles_in[row + j] for j in range(MIX_GROUP)])
        for j in range(MIX_GROUP):
            scale = lane_part[...] * (plane_part[pl.ds(row + j, 1), :] * columns[:, j : j + 1])
            done = tiles[j] * scale
            tiles_out[row + j] = done
            total += jnp.sum((done * done).reshape(N // 8, 8, N), axis=0)
        turning[...] = pltpu.roll(columns, N - MIX_GROUP, 1)
        each(MIX_GROUP, lambda j: store(row + j).start())
        return total

    total = lax.fori_loop(0, N // MIX_GROUP, turn, jnp.zeros((8, N), F32))
    squares[...] = jnp.broadcast_to(total[None], squares.shape)
    last = pltpu.make_async_copy(squares, out_ref.at[:, pl.ds(N, 8)], squares_sem)
    last.start()
    each(N, lambda row: store(row).wait())
    last.wait()


def finish_kernel(in_ref, out_ref, held, squares, squares_sem, in_sem, out_sem):
    def load(piece):
        part = pl.ds(piece * PIECE, PIECE)
        return pltpu.make_async_copy(in_ref.at[part, pl.ds(0, N)], held.at[part], in_sem.at[piece])

    def store(plane):
        columns = pl.ds(pl.multiple_of(plane * N, N), N)
        return pltpu.make_async_copy(held.at[plane], out_ref.at[:, columns], out_sem.at[plane])

    squares_load = pltpu.make_async_copy(in_ref.at[:, pl.ds(N, 8)], squares, squares_sem)
    squares_load.start()
    each(N // PIECE, lambda piece: load(piece).start())
    squares_load.wait()
    total = jnp.sum(jnp.sum(squares[...], axis=0))
    mean_square = total / jnp.float32(N * N * N * N)
    scale = lax.rsqrt(jnp.full((8, N), mean_square + 1e-06, F32))

    def piece_step(piece):
        load(piece).wait()
        for j in range(PIECE):
            plane = piece * PIECE + j
            held[plane] = held[plane] * scale[0:1]
            store(plane).start()

    each(N // PIECE, piece_step)
    each(N, lambda plane: store(plane).wait())


def local(initial_state, edge_list, couplings, gates_low, gates_mid, gates_high, top_gate):
    edges = edge_list.T
    couplings = couplings.reshape(1, -1)
    hbm = pl.BlockSpec(memory_space=pltpu.HBM)
    square = pltpu.VMEM((N, N), F32)
    cube = pltpu.VMEM((N, N, N), F32)
    pitched = pltpu.VMEM((N * PITCH, N), F32)
    gates = pltpu.VMEM((LAYERS, N, N), F32)
    small = [pltpu.VMEM(edges.shape, jnp.int32), pltpu.VMEM(couplings.shape, F32)]
    sems = lambda count: pltpu.SemaphoreType.DMA((count,))
    one_sem = pltpu.SemaphoreType.DMA

    evolved = pl.pallas_call(
        evolve_kernel,
        out_shape=jax.ShapeDtypeStruct((N, N, N), F32),
        in_specs=[hbm] * 6,
        out_specs=hbm,
        scratch_shapes=[
            pitched, pitched, pitched, *small, gates, gates, gates, square, square, square,
            pltpu.VMEM((3, 2 * N, 2 * N), BF16), sems(5), sems(N), sems(N),
        ],
        compiler_params=pltpu.CompilerParams(vmem_limit_bytes=VMEM_BYTES),
        name="evolve",
    )(edges, couplings, gates_low, gates_mid, gates_high, initial_state)

    gathered = lax.all_to_all(evolved, AXES, 0, 0, tiled=True)

    mixed = pl.pallas_call(
        mix_kernel,
        out_shape=jax.ShapeDtypeStruct((N, PITCH, N), F32),
        in_specs=[hbm] * 4,
        out_specs=hbm,
        scratch_shapes=[
            cube, cube, pltpu.VMEM((N, 8, N), F32), *small, square, square, square, square,
            pltpu.VMEM((2 * N, 2 * N), BF16), sems(3), sems(N), sems(N), one_sem,
        ],
        compiler_params=pltpu.CompilerParams(vmem_limit_bytes=VMEM_BYTES),
        name="mix",
    )(edges, couplings, top_gate, gathered)

    returned = lax.all_to_all(mixed, AXES, 0, 0, tiled=True)

    return pl.pallas_call(
        finish_kernel,
        out_shape=jax.ShapeDtypeStruct(initial_state.shape, F32),
        in_specs=[hbm],
        out_specs=hbm,
        scratch_shapes=[cube, pltpu.VMEM((N, 8, N), F32), one_sem, sems(N // PIECE), sems(N)],
        compiler_params=pltpu.CompilerParams(vmem_limit_bytes=VMEM_BYTES),
        name="finish",
    )(returned)


def solution(mesh):
    in_specs = (P(AXES, None), P(), P(), P(), P(), P(), P())
    return jax.shard_map(local, mesh=mesh, in_specs=in_specs, out_specs=P(AXES, None), check_vma=False)
```

time: 643 us -> 303 us (0.47)
  matrix products: 214 us -> 0 us
  local copies, waits for them, and re-layouts: 108 us -> 0 us
  Pallas kernels: 0 us -> 82.6 us
  blocking collectives: 279 us -> 220 us
  other arithmetic: 34.1 us -> 0 us
    dot_general x24 -> x0, matrix products: 214 us -> none  [the longest x6 79.5 us: local(): jnp.dot(gates_high[layer_index], amplitudes.reshape(high_rows, plane_size...]
    pallas_call x0 -> x3, Pallas kernels: none -> 82.6 us  [the longest x1 62.9 us: local(): pl.pallas_call(evolve_kernel, out_shape=jax.ShapeDtypeStruct((N, N, N), F...]
    psum x1 -> x0, blocking collectives: 63.9 us -> none  [local(): squares_total = lax.psum(jnp.sum(restored * restored), ('gx', 'gy'))]
    transpose x6 -> x0, local copies, waits for them, and re-layouts: 56 us -> none  [local(): jnp.matmul(gates_mid[layer_index][None], amplitudes.reshape(high_rows, bl...]
    reshape x2 -> x0, local copies, waits for them, and re-layouts: 36.1 us -> none  [the longest x1 18.1 us: local(): amplitudes.reshape(1, high_rows, plane_size)]
    unnamed x17 -> x0, local copies, waits for them, and re-layouts: 15.5 us -> none
    div x1 -> x0, other arithmetic: 13.1 us -> none  [local(): return restored / jnp.sqrt(mean_square + 1e-06)]
    reduce_sum x1 -> x0, other arithmetic: 11 us -> none  [local(): squares_total = lax.psum(jnp.sum(restored * restored), ('gx', 'gy'))]
where the time goes in v1:
time: 303 us
  blocking collectives  220 us (73%)
  Pallas kernels  82.6 us (27%)
    all_to_all x1, blocking collectives, local(): gathered = lax.all_to_all(evolved, AXES, 0, 0, tiled=True)  110 us
    all_to_all x1, blocking collectives, local(): returned = lax.all_to_all(mixed, AXES, 0, 0, tiled=True)  110 us
    pallas_call x1, Pallas kernels, local(): pl.pallas_call(evolve_kernel, out_shape=jax.ShapeDtypeStruct((N, N, N), F...  62.9 us
    pallas_call x1, Pallas kernels, local(): pl.pallas_call(mix_kernel, out_shape=jax.ShapeDtypeStruct((N, PITCH, N),...  11.9 us
    pallas_call x1, Pallas kernels, local(): pl.pallas_call(finish_kernel, out_shape=jax.ShapeDtypeStruct(initial_stat...  7.73 us

profile of v1, /device:TPU:1, one launch (start us, length us, event | category | flops | bytes accessed | tf_op | source)
XLA Modules:
  0.0 303.0 jit_solution(5098154564695703616)
XLA Ops:
  0.0 62.9 %evolve.1 = f32[128,128,128]{2,1,0:T(8,128)} custom-call(s32[2,56]{1,0:T(2,128)} %bitcast.2, f32[1,56]{1,0:T(1,128)} %bitcast.4, f32[6,128,128]{2,1,0:T(8,128)} %low_hbm.1, f32[6,128,128]{2,1,0:T(8,128)} %mid_hbm.1, f32[6,128,128]{2,1,0:T(8,128)} %high_hbm.1, f32[128,16384]{1,0:T(8,128)} %state_ref.1), custom_call_target="tpu_custom_call" | custom-call | tf_op jit(solution)/shard_map/evolve/pallas_call | solution.py:302
  62.9 110.2 %all_to_all.10.in_ref = f32[128,128,128]{2,1,0:T(8,128)} all-to-all(f32[128,128,128]{2,1,0:T(8,128)} %evolve.1), channel_id=1, replica_groups=mesh['gx'=16,'gy'=8] {'gx','gy'}, dimensions={0} | all-to-all | bytes 16777216 | tf_op jit(solution)/shard_map/all_to_all | solution.py:315
  173.1 11.9 %mix.1 = f32[128,136,128]{2,1,0:T(8,128)} custom-call(s32[2,56]{1,0:T(2,128)} %bitcast.3, f32[1,56]{1,0:T(1,128)} %bitcast.5, f32[128,128]{1,0:T(8,128)} %top_hbm.1, f32[128,128,128]{2,1,0:T(8,128)} %all_to_all.10.in_ref), custom_call_target="tpu_custom_call" | custom-call | tf_op jit(solution)/shard_map/mix/pallas_call | solution.py:317
  185.0 110.1 %all_to_all.11.in_ref = f32[128,136,128]{2,1,0:T(8,128)} all-to-all(f32[128,136,128]{2,1,0:T(8,128)} %mix.1), channel_id=1, replica_groups=mesh['gx'=16,'gy'=8] {'gx','gy'}, dimensions={0} | all-to-all | bytes 17825792 | tf_op jit(solution)/shard_map/all_to_all | solution.py:330
  295.1 7.7 %finish.1 = f32[128,16384]{1,0:T(8,128)} custom-call(f32[128,136,128]{2,1,0:T(8,128)} %all_to_all.11.in_ref), custom_call_target="tpu_custom_call" | custom-call | tf_op jit(solution)/shard_map/finish/pallas_call | solution.py:332

commit v2 on v1

v2 whole, which is shorter than its diff:
```python
import jax
import jax.numpy as jnp
from jax import lax
from jax.experimental import pallas as pl
from jax.experimental.pallas import tpu as pltpu
from jax.sharding import PartitionSpec as P

HIGHEST = lax.Precision.HIGHEST
F32 = jnp.float32
BF16 = jnp.bfloat16
N = 128
BITS = 7
LAYERS = 6
AXES = ("gx", "gy")
GROUP = 32
PITCH = N + 8
MIX_GROUP = 32


def mm(a, b):
    return lax.dot_general(a, b, (((1,), (0,)), ((), ())), preferred_element_type=F32)


def mm_nt_exact(a, b):
    return lax.dot_general(
        a, b, (((1,), (1,)), ((), ())), precision=HIGHEST, preferred_element_type=F32
    )


def iota(axis):
    return lax.broadcasted_iota(jnp.int32, (N, N), axis)


def split(x):
    high = x.astype(BF16)
    low = (x - high.astype(F32)).astype(BF16)
    return high, low


def left_pack(gate):
    high, low = split(gate)
    return jnp.concatenate(
        [jnp.concatenate([high, high], axis=1), jnp.concatenate([low, low], axis=1)], axis=0
    )


def right_pack(gate):
    high, low = split(gate.T)
    row = jnp.concatenate([high, low], axis=1)
    return jnp.concatenate([row, row], axis=0)


def left_gate(pack, tiles):
    out = []
    for i in range(0, len(tiles), 2):
        high, low = split(jnp.concatenate(tiles[i : i + 2], axis=1))
        both = mm(pack, jnp.concatenate([high, low], axis=0))
        both = both[:N] + both[N:]
        out += [both[:, :N], both[:, N:]]
    return out


def right_gate(pack, tiles):
    out = []
    for i in range(0, len(tiles), 2):
        high, low = split(jnp.concatenate(tiles[i : i + 2], axis=0))
        both = mm(jnp.concatenate([high, low], axis=1), pack)
        both = both[:, :N] + both[:, N:]
        out += [both[:N], both[N:]]
    return out


def spins(start, value):
    qubit = iota(1)
    inside = (qubit >= start) & (qubit < start + BITS)
    shift = jnp.clip(start + BITS - 1 - qubit, 0, BITS - 1)
    bit = jnp.right_shift(value, shift) & 1
    return jnp.where(inside, 1 - 2 * bit, 0).astype(F32)


def coupling_matrix(edge_ref, coupling_ref):
    names = lax.broadcasted_iota(jnp.int32, (N, edge_ref.shape[1]), 0)
    first = (edge_ref[0:1, :] == names).astype(F32) * coupling_ref[...]
    second = (edge_ref[1:2, :] == names).astype(F32)
    one_way = mm_nt_exact(first, second)
    return one_way + one_way.T


def flat_position():
    return lax.axis_index("gx") * lax.axis_size("gy") + lax.axis_index("gy")


def pieces_of(x):
    first = x.astype(BF16)
    rest = x - first.astype(F32)
    second = rest.astype(BF16)
    return [first, second, (rest - second.astype(F32)).astype(BF16)]


def spin_form(fields, spin_sets):
    left = jnp.concatenate([part for field in fields for part in pieces_of(field)], axis=1)
    right = jnp.concatenate([spin_set.astype(BF16) for spin_set in spin_sets for _ in range(3)], axis=1)
    return lax.dot_general(left, right, (((1,), (1,)), ((), ())), preferred_element_type=F32)


def pair_factors(matrix, fixed, rows, planes, lanes):
    every = jnp.concatenate([rows, planes, lanes, fixed], axis=0).astype(BF16)
    fields = mm(every, jnp.concatenate(pieces_of(matrix), axis=1))
    fields = fields[:, :N] + fields[:, N : 2 * N] + fields[:, 2 * N :]
    row_field, plane_field, lane_field, fixed_field = (fields[i * N : (i + 1) * N] for i in range(4))
    row_energy = jnp.sum((0.5 * row_field + fixed_field) * rows + 0.5 * fixed_field * fixed, axis=1, keepdims=True)
    plane_energy = jnp.sum((0.5 * plane_field + fixed_field) * planes, axis=1, keepdims=True)
    lane_energy = jnp.sum((0.5 * lane_field + fixed_field) * lanes, axis=1, keepdims=True)
    across = jnp.broadcast_to(lane_energy, (N, N)).T
    over_lanes = jnp.exp(spin_form([row_field], [lanes]) + row_energy)
    over_rows = jnp.exp(spin_form([row_field], [planes]))
    over_planes = jnp.exp(spin_form([plane_field], [lanes]) + (plane_energy + across))
    return over_lanes, over_rows, over_planes


def plane_tile(plane):
    return pl.ds(pl.multiple_of(plane * PITCH, 8), N)


def row_tile(row):
    return pl.ds(row, N, stride=PITCH)


def each(count, body):
    def step(i, c):
        body(i)
        return c

    lax.fori_loop(0, count, step, 0)


def sweep(body):
    each(N // GROUP, lambda i: body(i * GROUP))


def start_copies(sem, *pairs):
    copies = [pltpu.make_async_copy(source, target, sem.at[i]) for i, (source, target) in enumerate(pairs)]
    for copy in copies:
        copy.start()
    return copies


def evolve_kernel(edge_hbm, coupling_hbm, low_hbm, mid_hbm, high_hbm, top_hbm, state_ref,
                  out_ref, mix_factors_ref, mix_packs_ref,
                  landed, by_plane, by_row, factor, row_factor, edge_ref, coupling_ref, low_ref, mid_ref, high_ref, top_ref,
                  lane_part, plane_part, turning, packs, small_sem, in_sem, out_sem):
    def load(group):
        columns = pl.ds(pl.multiple_of(group * GROUP * N, GROUP * N), GROUP * N)
        return pltpu.make_async_copy(state_ref.at[:, columns], landed.at[:, columns], in_sem.at[group])

    def store(row):
        return pltpu.make_async_copy(by_row.at[plane_tile(row)], out_ref.at[:, row], out_sem)

    small = start_copies(
        small_sem,
        (edge_hbm, edge_ref), (coupling_hbm, coupling_ref),
        (high_hbm, high_ref), (low_hbm, low_ref), (mid_hbm, mid_ref), (top_hbm, top_ref),
    )
    each(N // GROUP, lambda group: load(group).start())
    for copy in small[:2]:
        copy.wait()
    matrix = coupling_matrix(edge_ref, coupling_ref)
    lane_part[...], turning[...], plane_part[...] = pair_factors(
        matrix,
        spins(0, flat_position()),
        spins(BITS, iota(0)),
        spins(2 * BITS, iota(0)),
        spins(3 * BITS, iota(0)),
    )
    for copy in small[2:]:
        copy.wait()
    packs[0] = left_pack(high_ref[0])
    packs[1] = right_pack(low_ref[0])

    def first(plane):
        load(plane // GROUP).wait()
        columns = turning[...]
        tiles = []
        for j in range(GROUP):
            scale = lane_part[...] * (plane_part[pl.ds(plane + j, 1), :] * columns[:, j : j + 1])
            factor[plane_tile(plane + j)] = scale
            tiles.append(landed[:, pl.ds(pl.multiple_of((plane + j) * N, N), N)] * scale)
        turning[...] = pltpu.roll(columns, N - GROUP, 1)
        tiles = right_gate(packs[1], left_gate(packs[0], tiles))
        for j in range(GROUP):
            by_plane[plane_tile(plane + j)] = tiles[j]

    sweep(first)

    for layer in range(1, LAYERS):
        rows_now = layer % 2 == 1
        across = mid_ref if rows_now else high_ref
        packs[0] = left_pack(across[layer - 1])
        packs[1] = left_pack(across[layer])
        packs[2] = right_pack(low_ref[layer])
        source, target = (by_plane, by_row) if rows_now else (by_row, by_plane)

        def middle(index, layer=layer, rows_now=rows_now, source=source, target=target):
            tiles = left_gate(packs[0], [source[row_tile(index + j)] for j in range(GROUP)])
            for j in range(GROUP):
                if rows_now and layer > 1:
                    scale = row_factor[plane_tile(index + j)]
                elif rows_now:
                    scale = factor[row_tile(index + j)]
                    row_factor[plane_tile(index + j)] = scale
                else:
                    scale = factor[plane_tile(index + j)]
                tiles[j] = tiles[j] * scale
            tiles = right_gate(packs[2], left_gate(packs[1], tiles))
            for j in range(GROUP):
                target[plane_tile(index + j)] = tiles[j]
            if layer == LAYERS - 1:
                each(GROUP, lambda j: store(index + j).start())

        sweep(middle)

    mix_packs_ref[0] = left_pack(top_ref[...])
    mix_packs_ref[1] = left_pack(high_ref[LAYERS - 1])
    mix_factors_ref[0], mix_factors_ref[1], mix_factors_ref[2] = pair_factors(
        coupling_matrix(edge_ref, coupling_ref),
        spins(2 * BITS, flat_position()),
        spins(BITS, iota(0)),
        spins(0, iota(0)),
        spins(3 * BITS, iota(0)),
    )
    pltpu.make_async_copy(landed, landed, out_sem).wait()


def mix_kernel(factors_ref, packs_ref, in_ref, out_ref, turned, turning):
    turning[...] = factors_ref[1]

    def top(i):
        tiles = []
        for j in range(0, MIX_GROUP, 8):
            rows = pl.ds(pl.multiple_of(i * MIX_GROUP + j, 8), 8)
            block = jnp.swapaxes(in_ref[:, rows, :].reshape(N // 8, 8, 8, N), 1, 2)
            tiles += [block[:, k].reshape(N, N) for k in range(8)]
        tiles = left_gate(packs_ref[0], tiles)
        for j in range(MIX_GROUP):
            turned[plane_tile(i * MIX_GROUP + j)] = tiles[j]

    each(N // MIX_GROUP, top)

    def high(i, total):
        device = i * GROUP
        columns = turning[...]
        tiles = left_gate(packs_ref[1], [turned[row_tile(device + j)] for j in range(GROUP)])
        for j in range(GROUP):
            scale = factors_ref[0] * (factors_ref[2, pl.ds(device + j, 1), :] * columns[:, j : j + 1])
            final = tiles[j] * scale
            out_ref[device + j, :N, :] = final
            total += jnp.sum((final * final).reshape(N // 8, 8, N), axis=0)
        turning[...] = pltpu.roll(columns, N - GROUP, 1)
        return total

    total = lax.fori_loop(0, N // GROUP, high, jnp.zeros((8, N), F32))
    out_ref[:, N:, :] = jnp.broadcast_to(total[None], (N, PITCH - N, N))


def finish_kernel(in_ref, out_ref, held, out_sem):
    def store(block):
        rows = pl.ds(pl.multiple_of(block * 8, 8), 8)
        return pltpu.make_async_copy(held.at[rows], out_ref.at[rows], out_sem.at[block])

    total = lax.fori_loop(0, N, lambda m, c: c + in_ref[m, pl.ds(N, 8), :], jnp.zeros((8, N), F32), unroll=8)
    mean_square = jnp.sum(total) / jnp.float32(N * N * N * N)
    scale = lax.rsqrt(jnp.full((8, N), mean_square + 1e-06, F32))

    def rows_step(block):
        rows = pl.ds(pl.multiple_of(block * 8, 8), 8)
        for m in range(N):
            held[rows, m * N : (m + 1) * N] = in_ref[m, rows, :] * scale
        store(block).start()

    each(N // 8, rows_step)
    each(N // 8, lambda block: store(block).wait())


def local(initial_state, edge_list, couplings, gates_low, gates_mid, gates_high, top_gate):
    edges = edge_list.T
    couplings = couplings.reshape(1, -1)
    vmem = pl.BlockSpec(memory_space=pltpu.VMEM)
    hbm = pl.BlockSpec(memory_space=pltpu.HBM)
    square = pltpu.VMEM((N, N), F32)
    pitched = pltpu.VMEM((N * PITCH, N), F32)
    flat = pltpu.VMEM((N, N * N), F32)
    one_sem = pltpu.SemaphoreType.DMA
    gates = pltpu.VMEM((LAYERS, N, N), F32)
    small = [pltpu.VMEM(edges.shape, jnp.int32), pltpu.VMEM(couplings.shape, F32)]
    sems = lambda count: pltpu.SemaphoreType.DMA((count,))

    evolved, mix_factors, mix_packs = pl.pallas_call(
        evolve_kernel,
        out_shape=[
            jax.ShapeDtypeStruct((N, N, N), F32),
            jax.ShapeDtypeStruct((3, N, N), F32),
            jax.ShapeDtypeStruct((2, 2 * N, 2 * N), BF16),
        ],
        in_specs=[hbm] * 7,
        out_specs=[hbm, vmem, vmem],
        scratch_shapes=[
            flat, pitched, pitched, pitched, pitched, *small, gates, gates, gates, square, square, square, square,
            pltpu.VMEM((3, 2 * N, 2 * N), BF16), sems(6), sems(N // GROUP), one_sem,
        ],
        compiler_params=pltpu.CompilerParams(vmem_limit_bytes=60 * 2**20),
        name="evolve",
    )(edges, couplings, gates_low, gates_mid, gates_high, top_gate, initial_state)

    gathered = lax.all_to_all(evolved, AXES, 0, 0, tiled=True)

    mixed = pl.pallas_call(
        mix_kernel,
        out_shape=jax.ShapeDtypeStruct((N, PITCH, N), F32),
        in_specs=[vmem] * 3,
        out_specs=vmem,
        scratch_shapes=[pitched, square],
        compiler_params=pltpu.CompilerParams(vmem_limit_bytes=28 * 2**20),
        name="mix",
    )(mix_factors, mix_packs, gathered)

    returned = lax.all_to_all(mixed, AXES, 0, 0, tiled=True)

    return pl.pallas_call(
        finish_kernel,
        out_shape=jax.ShapeDtypeStruct(initial_state.shape, F32),
        in_specs=[vmem],
        out_specs=hbm,
        scratch_shapes=[flat, sems(N // 8)],
        compiler_params=pltpu.CompilerParams(vmem_limit_bytes=32 * 2**20),
        name="finish",
    )(returned)


def solution(mesh):
    in_specs = (P(AXES, None), P(), P(), P(), P(), P(), P())
    return jax.shard_map(local, mesh=mesh, in_specs=in_specs, out_specs=P(AXES, None), check_vma=False)
```

time: 303 us -> 288 us (0.950)
  Pallas kernels: 82.6 us -> 67.6 us
    pallas_call x1, Pallas kernels: 62.9 us -> 55.7 us  [local(): pl.pallas_call(evolve_kernel, out_shape=[jax.ShapeDtypeStruct((N, N, N),...]
    pallas_call x1, Pallas kernels: 7.73 us -> 3.72 us  [local(): pl.pallas_call(finish_kernel, out_shape=jax.ShapeDtypeStruct(initial_stat...]
    pallas_call x1, Pallas kernels: 11.9 us -> 8.17 us  [local(): pl.pallas_call(mix_kernel, out_shape=jax.ShapeDtypeStruct((N, PITCH, N),...]
where the time goes in v2:
time: 288 us
  blocking collectives  220 us (76%)
  Pallas kernels  67.6 us (23%)
    all_to_all x1, blocking collectives, local(): gathered = lax.all_to_all(evolved, AXES, 0, 0, tiled=True)  110 us
    all_to_all x1, blocking collectives, local(): returned = lax.all_to_all(mixed, AXES, 0, 0, tiled=True)  110 us
    pallas_call x1, Pallas kernels, local(): pl.pallas_call(evolve_kernel, out_shape=[jax.ShapeDtypeStruct((N, N, N),...  55.7 us
    pallas_call x1, Pallas kernels, local(): pl.pallas_call(mix_kernel, out_shape=jax.ShapeDtypeStruct((N, PITCH, N),...  8.17 us

profile of v2, /device:TPU:1, one launch (start us, length us, event | category | flops | bytes accessed | tf_op | source)
XLA Modules:
  0.0 287.7 jit_solution(623685819065545361)
XLA Ops:
  0.0 55.7 %evolve.1 = (f32[128,128,128]{2,1,0:T(8,128)}, f32[3,128,128]{2,1,0:T(8,128)}, bf16[2,256,256]{2,1,0:T(8,128)(2,1)}) custom-call(s32[2,56]{1,0:T(2,128)} %bitcast.2, f32[1,56]{1,0:T(1,128)} %bitcast.3, f32[6,128,128]{2,1,0:T(8,128)} %low_hbm.1, f32[6,128,128]{2,1,0:T(8,128)} %mid_hbm.1, f32[6,128,128]{2,1,0:T(8,128)} %high_hbm.1, f32[128,128]{1,0:T(8,128)} %top_hbm.1, ...), custom_call_target="tpu_custom_call" | custom-call | tf_op jit(solution)/shard_map/evolve/pallas_call | solution.py:297
  55.7 0.0 copy-start
  55.8 0.0 copy-start.1
  55.8 110.1 %all_to_all.10.in_ref = f32[128,128,128]{2,1,0:T(8,128)S(1)} all-to-all(f32[128,128,128]{2,1,0:T(8,128)} %get-tuple-element.10), channel_id=1, replica_groups=mesh['gx'=16,'gy'=8] {'gx','gy'}, dimensions={0} | all-to-all | bytes 16777216 | tf_op jit(solution)/shard_map/all_to_all | solution.py:314
  165.8 0.0 copy-done
  165.8 0.0 copy-done.1
  165.8 8.2 %mix.1 = f32[128,136,128]{2,1,0:T(8,128)S(1)} custom-call(f32[3,128,128]{2,1,0:T(8,128)S(1)} %copy-done.1, bf16[2,256,256]{2,1,0:T(8,128)(2,1)S(1)} %copy-done, f32[128,128,128]{2,1,0:T(8,128)S(1)} %all_to_all.10.in_ref), custom_call_target="tpu_custom_call" | custom-call | tf_op jit(solution)/shard_map/mix/pallas_call | solution.py:316
  174.0 109.8 %all_to_all.11.in_ref = f32[128,136,128]{2,1,0:T(8,128)S(1)} all-to-all(f32[128,136,128]{2,1,0:T(8,128)S(1)} %mix.1), channel_id=1, replica_groups=mesh['gx'=16,'gy'=8] {'gx','gy'}, dimensions={0} | all-to-all | bytes 17825792 | tf_op jit(solution)/shard_map/all_to_all | solution.py:326
  283.8 3.7 %finish.1 = f32[128,16384]{1,0:T(8,128)} custom-call(f32[128,136,128]{2,1,0:T(8,128)S(1)} %all_to_all.11.in_ref), custom_call_target="tpu_custom_call" | custom-call | tf_op jit(solution)/shard_map/finish/pallas_call | solution.py:328
Async XLA Ops:
  55.7 110.1 %copy-start = (bf16[2,256,256]{2,1,0:T(8,128)(2,1)S(1)}, bf16[2,256,256]{2,1,0:T(8,128)(2,1)}, u32[]{:S(2)}) copy-start(bf16[2,256,256]{2,1,0:T(8,128)(2,1)} %get-tuple-element.9.packs_ref) | copy-start | bytes 786436
  55.8 110.1 %copy-start.1 = (f32[3,128,128]{2,1,0:T(8,128)S(1)}, f32[3,128,128]{2,1,0:T(8,128)}, u32[]{:S(2)}) copy-start(f32[3,128,128]{2,1,0:T(8,128)} %get-tuple-element.8.factors_ref) | copy-start | bytes 589828

commit v3 on v2

--- a/solution.py
+++ b/solution.py
@@ -12,9 +12,11 @@
 BITS = 7
 LAYERS = 6
 AXES = ("gx", "gy")
+EXCHANGE = ("gy", "gx")
 GROUP = 32
-PITCH = N + 8
-MIX_GROUP = 32
+WIDE_GROUP = 64
+PITCH = N + 1
+BLOCK = N + 8
 
 
 def mm(a, b):
@@ -86,8 +88,12 @@
     return one_way + one_way.T
 
 
-def flat_position():
-    return lax.axis_index("gx") * lax.axis_size("gy") + lax.axis_index("gy")
+def flat_position(axes):
+    return lax.axis_index(axes[0]) * lax.axis_size(axes[1]) + lax.axis_index(axes[1])
+
+
+def exchange_order(value):
+    return lax.rem(value, lax.axis_size("gx")) * lax.axis_size("gy") + lax.div(value, lax.axis_size("gx"))
 
 
 def pieces_of(x):
@@ -119,7 +125,7 @@
 
 
 def plane_tile(plane):
-    return pl.ds(pl.multiple_of(plane * PITCH, 8), N)
+    return pl.ds(plane * PITCH, N)
 
 
 def row_tile(row):
@@ -134,8 +140,15 @@
     lax.fori_loop(0, count, step, 0)
 
 
-def sweep(body):
-    each(N // GROUP, lambda i: body(i * GROUP))
+def sweep(body, group):
+    each(N // group, lambda i: body(i * group))
+
+
+def reorder(gate):
+    to_place = (exchange_order(iota(0)) == iota(1)).astype(BF16)
+    rows = sum(mm(to_place, part) for part in pieces_of(gate))
+    both = sum(mm(to_place, part) for part in pieces_of(rows.T))
+    return both.T
 
 
 def start_copies(sem, *pairs):
@@ -147,27 +160,28 @@
 
 def evolve_kernel(edge_hbm, coupling_hbm, low_hbm, mid_hbm, high_hbm, top_hbm, state_ref,
                   out_ref, mix_factors_ref, mix_packs_ref,
-                  landed, by_plane, by_row, factor, row_factor, edge_ref, coupling_ref, low_ref, mid_ref, high_ref, top_ref,
+                  landed, leaving, by_plane, by_row, factor, row_factor, edge_ref, coupling_ref, low_ref, mid_ref, high_ref, top_ref,
                   lane_part, plane_part, turning, packs, small_sem, in_sem, out_sem):
     def load(group):
         columns = pl.ds(pl.multiple_of(group * GROUP * N, GROUP * N), GROUP * N)
         return pltpu.make_async_copy(state_ref.at[:, columns], landed.at[:, columns], in_sem.at[group])
 
     def store(row):
-        return pltpu.make_async_copy(by_row.at[plane_tile(row)], out_ref.at[:, row], out_sem)
-
+        return pltpu.make_async_copy(leaving.at[row], out_ref.at[:, row], out_sem)
+
+    load(0).start()
     small = start_copies(
         small_sem,
         (edge_hbm, edge_ref), (coupling_hbm, coupling_ref),
         (high_hbm, high_ref), (low_hbm, low_ref), (mid_hbm, mid_ref), (top_hbm, top_ref),
     )
-    each(N // GROUP, lambda group: load(group).start())
+    each(N // GROUP - 1, lambda group: load(group + 1).start())
     for copy in small[:2]:
         copy.wait()
     matrix = coupling_matrix(edge_ref, coupling_ref)
     lane_part[...], turning[...], plane_part[...] = pair_factors(
         matrix,
-        spins(0, flat_position()),
+        spins(0, flat_position(AXES)),
         spins(BITS, iota(0)),
         spins(2 * BITS, iota(0)),
         spins(3 * BITS, iota(0)),
@@ -190,7 +204,7 @@
         for j in range(GROUP):
             by_plane[plane_tile(plane + j)] = tiles[j]
 
-    sweep(first)
+    sweep(first, GROUP)
 
     for layer in range(1, LAYERS):
         rows_now = layer % 2 == 1
@@ -200,9 +214,12 @@
         packs[2] = right_pack(low_ref[layer])
         source, target = (by_plane, by_row) if rows_now else (by_row, by_plane)
 
-        def middle(index, layer=layer, rows_now=rows_now, source=source, target=target):
-            tiles = left_gate(packs[0], [source[row_tile(index + j)] for j in range(GROUP)])
-            for j in range(GROUP):
+        ending = layer == LAYERS - 1
+        group = GROUP if ending else WIDE_GROUP
+
+        def middle(index, layer=layer, rows_now=rows_now, source=source, target=target, ending=ending, group=group):
+            tiles = left_gate(packs[0], [source[row_tile(index + j)] for j in range(group)])
+            for j in range(group):
                 if rows_now and layer > 1:
                     scale = row_factor[plane_tile(index + j)]
                 elif rows_now:
@@ -212,20 +229,23 @@
                     scale = factor[plane_tile(index + j)]
                 tiles[j] = tiles[j] * scale
             tiles = right_gate(packs[2], left_gate(packs[1], tiles))
-            for j in range(GROUP):
-                target[plane_tile(index + j)] = tiles[j]
-            if layer == LAYERS - 1:
-                each(GROUP, lambda j: store(index + j).start())
-
-        sweep(middle)
-
-    mix_packs_ref[0] = left_pack(top_ref[...])
+            for j in range(group):
+                if ending:
+                    leaving[index + j] = tiles[j]
+                else:
+                    target[plane_tile(index + j)] = tiles[j]
+            if ending:
+                each(group, lambda j: store(index + j).start())
+
+        sweep(middle, group)
+
+    mix_packs_ref[0] = left_pack(reorder(top_ref[...]))
     mix_packs_ref[1] = left_pack(high_ref[LAYERS - 1])
     mix_factors_ref[0], mix_factors_ref[1], mix_factors_ref[2] = pair_factors(
         coupling_matrix(edge_ref, coupling_ref),
-        spins(2 * BITS, flat_position()),
+        spins(2 * BITS, flat_position(EXCHANGE)),
         spins(BITS, iota(0)),
-        spins(0, iota(0)),
+        spins(0, exchange_order(iota(0))),
         spins(3 * BITS, iota(0)),
     )
     pltpu.make_async_copy(landed, landed, out_sem).wait()
@@ -236,15 +256,15 @@
 
     def top(i):
         tiles = []
-        for j in range(0, MIX_GROUP, 8):
-            rows = pl.ds(pl.multiple_of(i * MIX_GROUP + j, 8), 8)
+        for j in range(0, WIDE_GROUP, 8):
+            rows = pl.ds(pl.multiple_of(i * WIDE_GROUP + j, 8), 8)
             block = jnp.swapaxes(in_ref[:, rows, :].reshape(N // 8, 8, 8, N), 1, 2)
             tiles += [block[:, k].reshape(N, N) for k in range(8)]
         tiles = left_gate(packs_ref[0], tiles)
-        for j in range(MIX_GROUP):
-            turned[plane_tile(i * MIX_GROUP + j)] = tiles[j]
-
-    each(N // MIX_GROUP, top)
+        for j in range(WIDE_GROUP):
+            turned[plane_tile(i * WIDE_GROUP + j)] = tiles[j]
+
+    each(N // WIDE_GROUP, top)
 
     def high(i, total):
         device = i * GROUP
@@ -259,7 +279,7 @@
         return total
 
     total = lax.fori_loop(0, N // GROUP, high, jnp.zeros((8, N), F32))
-    out_ref[:, N:, :] = jnp.broadcast_to(total[None], (N, PITCH - N, N))
+    out_ref[:, N:, :] = jnp.broadcast_to(total[None], (N, BLOCK - N, N))
 
 
 def finish_kernel(in_ref, out_ref, held, out_sem):
@@ -304,18 +324,18 @@
         in_specs=[hbm] * 7,
         out_specs=[hbm, vmem, vmem],
         scratch_shapes=[
-            flat, pitched, pitched, pitched, pitched, *small, gates, gates, gates, square, square, square, square,
+            flat, pltpu.VMEM((N, N, N), F32), pitched, pitched, pitched, pitched, *small, gates, gates, gates, square, square, square, square,
             pltpu.VMEM((3, 2 * N, 2 * N), BF16), sems(6), sems(N // GROUP), one_sem,
         ],
         compiler_params=pltpu.CompilerParams(vmem_limit_bytes=60 * 2**20),
         name="evolve",
     )(edges, couplings, gates_low, gates_mid, gates_high, top_gate, initial_state)
 
-    gathered = lax.all_to_all(evolved, AXES, 0, 0, tiled=True)
+    gathered = lax.all_to_all(evolved, EXCHANGE, 0, 0, tiled=True)
 
     mixed = pl.pallas_call(
         mix_kernel,
-        out_shape=jax.ShapeDtypeStruct((N, PITCH, N), F32),
+        out_shape=jax.ShapeDtypeStruct((N, BLOCK, N), F32),
         in_specs=[vmem] * 3,
         out_specs=vmem,
         scratch_shapes=[pitched, square],
@@ -323,7 +343,7 @@
         name="mix",
     )(mix_factors, mix_packs, gathered)
 
-    returned = lax.all_to_all(mixed, AXES, 0, 0, tiled=True)
+    returned = lax.all_to_all(mixed, EXCHANGE, 0, 0, tiled=True)
 
     return pl.pallas_call(
         finish_kernel,

time: 288 us -> 278 us (0.965)
  Pallas kernels: 67.6 us -> 61.1 us
  blocking collectives: 220 us -> 217 us
    pallas_call x1, Pallas kernels: 55.7 us -> 50.3 us  [local(): pl.pallas_call(evolve_kernel, out_shape=[jax.ShapeDtypeStruct((N, N, N),...]
where the time goes in v3:
time: 278 us
  blocking collectives  217 us (78%)
  Pallas kernels  61.1 us (22%)
    all_to_all x1, blocking collectives, local(): returned = lax.all_to_all(mixed, EXCHANGE, 0, 0, tiled=True)  109 us
    all_to_all x1, blocking collectives, local(): gathered = lax.all_to_all(evolved, EXCHANGE, 0, 0, tiled=True)  108 us
    pallas_call x1, Pallas kernels, local(): pl.pallas_call(evolve_kernel, out_shape=[jax.ShapeDtypeStruct((N, N, N),...  50.3 us
    pallas_call x1, Pallas kernels, local(): pl.pallas_call(mix_kernel, out_shape=jax.ShapeDtypeStruct((N, BLOCK, N),...  7.08 us

profile of v3, /device:TPU:1, one launch (start us, length us, event | category | flops | bytes accessed | tf_op | source)
XLA Modules:
  0.0 278.3 jit_solution(9889569139048619572)
XLA Ops:
  0.0 50.3 %evolve.1 = (f32[128,128,128]{2,1,0:T(8,128)}, f32[3,128,128]{2,1,0:T(8,128)}, bf16[2,256,256]{2,1,0:T(8,128)(2,1)}) custom-call(s32[2,56]{1,0:T(2,128)} %bitcast.2, f32[1,56]{1,0:T(1,128)} %bitcast.3, f32[6,128,128]{2,1,0:T(8,128)} %low_hbm.1, f32[6,128,128]{2,1,0:T(8,128)} %mid_hbm.1, f32[6,128,128]{2,1,0:T(8,128)} %high_hbm.1, f32[128,128]{1,0:T(8,128)} %top_hbm.1, ...), custom_call_target="tpu_custom_call" | custom-call | tf_op jit(solution)/shard_map/evolve/pallas_call | solution.py:317
  50.3 0.0 copy-start
  50.3 0.0 copy-start.1
  50.3 108.3 %all_to_all.10.in_ref = f32[128,128,128]{2,1,0:T(8,128)S(1)} all-to-all(f32[128,128,128]{2,1,0:T(8,128)} %get-tuple-element.10), channel_id=1, replica_groups=mesh['gx'=16,'gy'=8] {'gy','gx'}, dimensions={0} | all-to-all | bytes 16777216 | tf_op jit(solution)/shard_map/all_to_all | solution.py:334
  158.6 0.0 copy-done
  158.6 0.0 copy-done.1
  158.6 7.1 %mix.1 = f32[128,136,128]{2,1,0:T(8,128)S(1)} custom-call(f32[3,128,128]{2,1,0:T(8,128)S(1)} %copy-done.1, bf16[2,256,256]{2,1,0:T(8,128)(2,1)S(1)} %copy-done, f32[128,128,128]{2,1,0:T(8,128)S(1)} %all_to_all.10.in_ref), custom_call_target="tpu_custom_call" | custom-call | tf_op jit(solution)/shard_map/mix/pallas_call | solution.py:336
  165.7 108.7 %all_to_all.11.in_ref = f32[128,136,128]{2,1,0:T(8,128)S(1)} all-to-all(f32[128,136,128]{2,1,0:T(8,128)S(1)} %mix.1), channel_id=1, replica_groups=mesh['gx'=16,'gy'=8] {'gy','gx'}, dimensions={0} | all-to-all | bytes 17825792 | tf_op jit(solution)/shard_map/all_to_all | solution.py:346
  274.4 3.7 %finish.1 = f32[128,16384]{1,0:T(8,128)} custom-call(f32[128,136,128]{2,1,0:T(8,128)S(1)} %all_to_all.11.in_ref), custom_call_target="tpu_custom_call" | custom-call | tf_op jit(solution)/shard_map/finish/pallas_call | solution.py:348
Async XLA Ops:
  50.3 108.3 %copy-start = (bf16[2,256,256]{2,1,0:T(8,128)(2,1)S(1)}, bf16[2,256,256]{2,1,0:T(8,128)(2,1)}, u32[]{:S(2)}) copy-start(bf16[2,256,256]{2,1,0:T(8,128)(2,1)} %get-tuple-element.9.packs_ref) | copy-start | bytes 786436
  50.3 108.3 %copy-start.1 = (f32[3,128,128]{2,1,0:T(8,128)S(1)}, f32[3,128,128]{2,1,0:T(8,128)}, u32[]{:S(2)}) copy-start(f32[3,128,128]{2,1,0:T(8,128)} %get-tuple-element.8.factors_ref) | copy-start | bytes 589828

commit v4 on v3

--- a/solution.py
+++ b/solution.py
@@ -188,8 +188,15 @@
     )
     for copy in small[2:]:
         copy.wait()
-    packs[0] = left_pack(high_ref[0])
-    packs[1] = right_pack(low_ref[0])
+    packs[0, 0] = left_pack(high_ref[0])
+    packs[0, 1] = right_pack(low_ref[0])
+
+    def prepare(layer):
+        if layer < LAYERS:
+            across = mid_ref if layer % 2 == 1 else high_ref
+            packs[layer % 2, 0] = left_pack(across[layer - 1])
+            packs[layer % 2, 1] = left_pack(across[layer])
+            packs[layer % 2, 2] = right_pack(low_ref[layer])
 
     def first(plane):
         load(plane // GROUP).wait()
@@ -200,7 +207,8 @@
             factor[plane_tile(plane + j)] = scale
             tiles.append(landed[:, pl.ds(pl.multiple_of((plane + j) * N, N), N)] * scale)
         turning[...] = pltpu.roll(columns, N - GROUP, 1)
-        tiles = right_gate(packs[1], left_gate(packs[0], tiles))
+        tiles = right_gate(packs[0, 1], left_gate(packs[0, 0], tiles))
+        prepare(1)
         for j in range(GROUP):
             by_plane[plane_tile(plane + j)] = tiles[j]
 
@@ -208,17 +216,14 @@
 
     for layer in range(1, LAYERS):
         rows_now = layer % 2 == 1
-        across = mid_ref if rows_now else high_ref
-        packs[0] = left_pack(across[layer - 1])
-        packs[1] = left_pack(across[layer])
-        packs[2] = right_pack(low_ref[layer])
+        now = packs.at[layer % 2]
         source, target = (by_plane, by_row) if rows_now else (by_row, by_plane)
 
         ending = layer == LAYERS - 1
         group = GROUP if ending else WIDE_GROUP
 
-        def middle(index, layer=layer, rows_now=rows_now, source=source, target=target, ending=ending, group=group):
-            tiles = left_gate(packs[0], [source[row_tile(index + j)] for j in range(group)])
+        def middle(index, layer=layer, rows_now=rows_now, source=source, target=target, ending=ending, group=group, now=now):
+            tiles = left_gate(now[0], [source[row_tile(index + j)] for j in range(group)])
             for j in range(group):
                 if rows_now and layer > 1:
                     scale = row_factor[plane_tile(index + j)]
@@ -228,14 +233,14 @@
                 else:
                     scale = factor[plane_tile(index + j)]
                 tiles[j] = tiles[j] * scale
-            tiles = right_gate(packs[2], left_gate(packs[1], tiles))
+            tiles = right_gate(now[2], left_gate(now[1], tiles))
+            prepare(layer + 1)
             for j in range(group):
                 if ending:
                     leaving[index + j] = tiles[j]
+                    store(index + j).start()
                 else:
                     target[plane_tile(index + j)] = tiles[j]
-            if ending:
-                each(group, lambda j: store(index + j).start())
 
         sweep(middle, group)
 
@@ -267,18 +272,18 @@
     each(N // WIDE_GROUP, top)
 
     def high(i, total):
-        device = i * GROUP
+        device = i * WIDE_GROUP
         columns = turning[...]
-        tiles = left_gate(packs_ref[1], [turned[row_tile(device + j)] for j in range(GROUP)])
-        for j in range(GROUP):
+        tiles = left_gate(packs_ref[1], [turned[row_tile(device + j)] for j in range(WIDE_GROUP)])
+        for j in range(WIDE_GROUP):
             scale = factors_ref[0] * (factors_ref[2, pl.ds(device + j, 1), :] * columns[:, j : j + 1])
             final = tiles[j] * scale
             out_ref[device + j, :N, :] = final
             total += jnp.sum((final * final).reshape(N // 8, 8, N), axis=0)
-        turning[...] = pltpu.roll(columns, N - GROUP, 1)
+        turning[...] = pltpu.roll(columns, N - WIDE_GROUP, 1)
         return total
 
-    total = lax.fori_loop(0, N // GROUP, high, jnp.zeros((8, N), F32))
+    total = lax.fori_loop(0, N // WIDE_GROUP, high, jnp.zeros((8, N), F32))
     out_ref[:, N:, :] = jnp.broadcast_to(total[None], (N, BLOCK - N, N))
 
 
@@ -325,7 +330,7 @@
         out_specs=[hbm, vmem, vmem],
         scratch_shapes=[
             flat, pltpu.VMEM((N, N, N), F32), pitched, pitched, pitched, pitched, *small, gates, gates, gates, square, square, square, square,
-            pltpu.VMEM((3, 2 * N, 2 * N), BF16), sems(6), sems(N // GROUP), one_sem,
+            pltpu.VMEM((2, 3, 2 * N, 2 * N), BF16), sems(6), sems(N // GROUP), one_sem,
         ],
         compiler_params=pltpu.CompilerParams(vmem_limit_bytes=60 * 2**20),
         name="evolve",

time: 278 us -> 277 us (level)
  no operation moved by 1% of the time
where the time goes in v4:
time: 277 us
  blocking collectives  217 us (78%)
  Pallas kernels  59.5 us (21%)
    all_to_all x1, blocking collectives, local(): returned = lax.all_to_all(mixed, EXCHANGE, 0, 0, tiled=True)  109 us
    all_to_all x1, blocking collectives, local(): gathered = lax.all_to_all(evolved, EXCHANGE, 0, 0, tiled=True)  108 us
    pallas_call x1, Pallas kernels, local(): pl.pallas_call(evolve_kernel, out_shape=[jax.ShapeDtypeStruct((N, N, N),...  48.8 us
    pallas_call x1, Pallas kernels, local(): pl.pallas_call(mix_kernel, out_shape=jax.ShapeDtypeStruct((N, BLOCK, N),...  6.93 us

profile of v4, /device:TPU:1, one launch (start us, length us, event | category | flops | bytes accessed | tf_op | source)
XLA Modules:
  0.0 276.7 jit_solution(11394489680428474469)
XLA Ops:
  0.0 48.8 %evolve.1 = (f32[128,128,128]{2,1,0:T(8,128)}, f32[3,128,128]{2,1,0:T(8,128)}, bf16[2,256,256]{2,1,0:T(8,128)(2,1)}) custom-call(s32[2,56]{1,0:T(2,128)} %bitcast.2, f32[1,56]{1,0:T(1,128)} %bitcast.3, f32[6,128,128]{2,1,0:T(8,128)} %low_hbm.1, f32[6,128,128]{2,1,0:T(8,128)} %mid_hbm.1, f32[6,128,128]{2,1,0:T(8,128)} %high_hbm.1, f32[128,128]{1,0:T(8,128)} %top_hbm.1, ...), custom_call_target="tpu_custom_call" | custom-call | tf_op jit(solution)/shard_map/evolve/pallas_call | solution.py:322
  48.8 0.0 copy-start
  48.9 0.0 copy-start.1
  48.9 108.4 %all_to_all.10.in_ref = f32[128,128,128]{2,1,0:T(8,128)S(1)} all-to-all(f32[128,128,128]{2,1,0:T(8,128)} %get-tuple-element.10), channel_id=1, replica_groups=mesh['gx'=16,'gy'=8] {'gy','gx'}, dimensions={0} | all-to-all | bytes 16777216 | tf_op jit(solution)/shard_map/all_to_all | solution.py:339
  157.2 0.0 copy-done
  157.2 0.0 copy-done.1
  157.2 6.9 %mix.1 = f32[128,136,128]{2,1,0:T(8,128)S(1)} custom-call(f32[3,128,128]{2,1,0:T(8,128)S(1)} %copy-done.1, bf16[2,256,256]{2,1,0:T(8,128)(2,1)S(1)} %copy-done, f32[128,128,128]{2,1,0:T(8,128)S(1)} %all_to_all.10.in_ref), custom_call_target="tpu_custom_call" | custom-call | tf_op jit(solution)/shard_map/mix/pallas_call | solution.py:341
  164.2 108.7 %all_to_all.11.in_ref = f32[128,136,128]{2,1,0:T(8,128)S(1)} all-to-all(f32[128,136,128]{2,1,0:T(8,128)S(1)} %mix.1), channel_id=1, replica_groups=mesh['gx'=16,'gy'=8] {'gy','gx'}, dimensions={0} | all-to-all | bytes 17825792 | tf_op jit(solution)/shard_map/all_to_all | solution.py:351
  272.8 3.7 %finish.1 = f32[128,16384]{1,0:T(8,128)} custom-call(f32[128,136,128]{2,1,0:T(8,128)S(1)} %all_to_all.11.in_ref), custom_call_target="tpu_custom_call" | custom-call | tf_op jit(solution)/shard_map/finish/pallas_call | solution.py:353
Async XLA Ops:
  48.8 108.4 %copy-start = (bf16[2,256,256]{2,1,0:T(8,128)(2,1)S(1)}, bf16[2,256,256]{2,1,0:T(8,128)(2,1)}, u32[]{:S(2)}) copy-start(bf16[2,256,256]{2,1,0:T(8,128)(2,1)} %get-tuple-element.9.packs_ref) | copy-start | bytes 786436
  48.9 108.4 %copy-start.1 = (f32[3,128,128]{2,1,0:T(8,128)S(1)}, f32[3,128,128]{2,1,0:T(8,128)}, u32[]{:S(2)}) copy-start(f32[3,128,128]{2,1,0:T(8,128)} %get-tuple-element.8.factors_ref) | copy-start | bytes 589828

commit v5 on v4

--- a/solution.py
+++ b/solution.py
@@ -312,7 +312,7 @@
     vmem = pl.BlockSpec(memory_space=pltpu.VMEM)
     hbm = pl.BlockSpec(memory_space=pltpu.HBM)
     square = pltpu.VMEM((N, N), F32)
-    pitched = pltpu.VMEM((N * PITCH, N), F32)
+    pitched = pltpu.VMEM((N * (PITCH + 1), N), F32)
     flat = pltpu.VMEM((N, N * N), F32)
     one_sem = pltpu.SemaphoreType.DMA
     gates = pltpu.VMEM((LAYERS, N, N), F32)

time: 277 us -> 277 us (level)
  no operation moved by 1% of the time
where the time goes in v5:
time: 277 us
  blocking collectives  217 us (78%)
  Pallas kernels  59.5 us (21%)
    all_to_all x1, blocking collectives, local(): returned = lax.all_to_all(mixed, EXCHANGE, 0, 0, tiled=True)  109 us
    all_to_all x1, blocking collectives, local(): gathered = lax.all_to_all(evolved, EXCHANGE, 0, 0, tiled=True)  108 us
    pallas_call x1, Pallas kernels, local(): pl.pallas_call(evolve_kernel, out_shape=[jax.ShapeDtypeStruct((N, N, N),...  48.8 us
    pallas_call x1, Pallas kernels, local(): pl.pallas_call(mix_kernel, out_shape=jax.ShapeDtypeStruct((N, BLOCK, N),...  6.93 us

profile of v5, /device:TPU:1, one launch (start us, length us, event | category | flops | bytes accessed | tf_op | source)
XLA Modules:
  0.0 276.7 jit_solution(13802921543250927208)
XLA Ops:
  0.0 48.8 %evolve.1 = (f32[128,128,128]{2,1,0:T(8,128)}, f32[3,128,128]{2,1,0:T(8,128)}, bf16[2,256,256]{2,1,0:T(8,128)(2,1)}) custom-call(s32[2,56]{1,0:T(2,128)} %bitcast.2, f32[1,56]{1,0:T(1,128)} %bitcast.3, f32[6,128,128]{2,1,0:T(8,128)} %low_hbm.1, f32[6,128,128]{2,1,0:T(8,128)} %mid_hbm.1, f32[6,128,128]{2,1,0:T(8,128)} %high_hbm.1, f32[128,128]{1,0:T(8,128)} %top_hbm.1, ...), custom_call_target="tpu_custom_call" | custom-call | tf_op jit(solution)/shard_map/evolve/pallas_call | solution.py:322
  48.8 0.0 copy-start
  48.9 0.0 copy-start.1
  48.9 108.4 %all_to_all.10.in_ref = f32[128,128,128]{2,1,0:T(8,128)S(1)} all-to-all(f32[128,128,128]{2,1,0:T(8,128)} %get-tuple-element.10), channel_id=1, replica_groups=mesh['gx'=16,'gy'=8] {'gy','gx'}, dimensions={0} | all-to-all | bytes 16777216 | tf_op jit(solution)/shard_map/all_to_all | solution.py:339
  157.2 0.0 copy-done
  157.2 0.0 copy-done.1
  157.2 6.9 %mix.1 = f32[128,136,128]{2,1,0:T(8,128)S(1)} custom-call(f32[3,128,128]{2,1,0:T(8,128)S(1)} %copy-done.1, bf16[2,256,256]{2,1,0:T(8,128)(2,1)S(1)} %copy-done, f32[128,128,128]{2,1,0:T(8,128)S(1)} %all_to_all.10.in_ref), custom_call_target="tpu_custom_call" | custom-call | tf_op jit(solution)/shard_map/mix/pallas_call | solution.py:341
  164.2 108.7 %all_to_all.11.in_ref = f32[128,136,128]{2,1,0:T(8,128)S(1)} all-to-all(f32[128,136,128]{2,1,0:T(8,128)S(1)} %mix.1), channel_id=1, replica_groups=mesh['gx'=16,'gy'=8] {'gy','gx'}, dimensions={0} | all-to-all | bytes 17825792 | tf_op jit(solution)/shard_map/all_to_all | solution.py:351
  272.8 3.7 %finish.1 = f32[128,16384]{1,0:T(8,128)} custom-call(f32[128,136,128]{2,1,0:T(8,128)S(1)} %all_to_all.11.in_ref), custom_call_target="tpu_custom_call" | custom-call | tf_op jit(solution)/shard_map/finish/pallas_call | solution.py:353
Async XLA Ops:
  48.8 108.4 %copy-start = (bf16[2,256,256]{2,1,0:T(8,128)(2,1)S(1)}, bf16[2,256,256]{2,1,0:T(8,128)(2,1)}, u32[]{:S(2)}) copy-start(bf16[2,256,256]{2,1,0:T(8,128)(2,1)} %get-tuple-element.9.packs_ref) | copy-start | bytes 786436
  48.9 108.4 %copy-start.1 = (f32[3,128,128]{2,1,0:T(8,128)S(1)}, f32[3,128,128]{2,1,0:T(8,128)}, u32[]{:S(2)}) copy-start(f32[3,128,128]{2,1,0:T(8,128)} %get-tuple-element.8.factors_ref) | copy-start | bytes 589828
